TPU v7x, 128 devices: a whole 4x4x4 slice. The times are simulated.
128 devices in a mesh: ctx: 16 (over x, y), head: 8 (over z, core).
Axes of the slice: x: 4, y: 4, z: 4, core: 2. Of those that a mesh axis runs over, the one named last changes fastest.
Arguments:
- q_rows: bfloat16 [16384, 8192], P(('ctx', 'head')), may hold values from -75 to 75
- key_rows: bfloat16 [16384, 1024], P('ctx', 'head'), may hold values from -6 to 6
- value_rows: bfloat16 [16384, 1024], P('ctx', 'head'), may hold values from -6 to 6
- doc_lengths: int32 [16], replicated, may hold values from 1 to 9216, 16384 in all
- window_widths: int32 [8], replicated, may hold values from 512 to 2048, as said below
- sink_widths: int32 [8], replicated, may hold values from 16 to 32, as said below
Outputs:
- attended: bfloat16 [16384, 8192], P('ctx', 'head')
Inputs may be any that keep to these rules, and one draw needn't show every extreme that they name: `doc_lengths`: each is at least 1; they sum to 16384; the longest equals 9216. `window_widths`: at least one KV head has a window of exactly 2048. `sink_widths`: at least one KV head has exactly 32 sink tokens.
All inputs are finite; a program needn't handle non-finite values.
Results may differ from a plain program's by a relative error of at most 0.004.
Values may be sent and summed in bfloat16 or wider, within the bound.
A program may use at most 128 MiB of HBM per device.

v0:
```python
import jax
import jax.numpy as jnp
from jax import lax
from jax.sharding import PartitionSpec as P

HD = 128
QPG = 8
WSPAN = 2
SINK_MAX = 32


def doc_index(positions, starts):
    return jnp.sum((positions[:, None] >= starts[None, :]).astype(jnp.int32), axis=1) - 1


def per_device(q_rows, key_rows, value_rows, doc_lengths, window_widths, sink_widths):
    queries = lax.all_to_all(q_rows, "head", split_axis=1, concat_axis=0, tiled=True)
    rows_here = key_rows.shape[0]
    groups = key_rows.shape[1] // HD
    shard_start = lax.axis_index("ctx") * rows_here
    first_group = lax.axis_index("head") * groups
    own_window = lax.dynamic_slice_in_dim(window_widths, first_group, groups)
    own_sink = lax.dynamic_slice_in_dim(sink_widths, first_group, groups)
    starts = jnp.cumsum(doc_lengths) - doc_lengths
    doc_count = doc_lengths.shape[0]
    query_pos = shard_start + jnp.arange(rows_here, dtype=jnp.int32)
    query_doc = doc_index(query_pos, starts)
    queries = queries.reshape(rows_here, groups, QPG, HD)
    score_scale = HD ** (-0.5)
    span = WSPAN * rows_here
    offsets = jnp.arange(SINK_MAX, dtype=jnp.int32)
    sink_pos = (starts[:, None] + offsets[None, :]).reshape(-1)
    sink_rank = jnp.tile(offsets, doc_count)
    sink_doc = jnp.repeat(jnp.arange(doc_count, dtype=jnp.int32), SINK_MAX)
    sink_live = sink_rank < jnp.repeat(doc_lengths, SINK_MAX)
    doc_ids = jnp.arange(doc_count, dtype=jnp.int32)
    query_first = jnp.sum(
        jnp.where(query_doc[:, None] == doc_ids[None, :], starts[None, :], 0), axis=1
    )
    wanted_sink = sink_live & (sink_doc >= query_doc[0]) & (sink_doc <= query_doc[-1])
    init = (
        jnp.full((groups, QPG, rows_here), -1e30, jnp.float32),
        jnp.zeros((groups, QPG, rows_here), jnp.float32),
        jnp.zeros((groups, QPG, rows_here, HD), jnp.float32),
    )
    piece_keys = lax.all_gather(key_rows, "ctx", axis=0, tiled=True)
    piece_values = lax.all_gather(value_rows, "ctx", axis=0, tiled=True)
    count = piece_keys.shape[0] // rows_here
    piece_keys = piece_keys.reshape(count, rows_here, groups, HD)
    piece_values = piece_values.reshape(count, rows_here, groups, HD)

    def one_shard(state, item):
        shard_keys, shard_values, number = item
        key_first = number * rows_here
        key_pos = key_first + jnp.arange(rows_here, dtype=jnp.int32)

        def compute(old):
            key_doc = doc_index(key_pos, starts)
            gap = query_pos[:, None] - key_pos[None, :]
            same = (key_doc[None, :] == query_doc[:, None]) & (gap >= 0)
            inside = gap[None] < own_window[:, None, None]
            early = (key_pos[None, :] - query_first[:, None])[None] < own_sink[:, None, None]
            mask = (same[None] & (inside | early))[:, None]
            scores = (
                jnp.einsum(
                    "qgjd,kgd->gjqk", queries, shard_keys, preferred_element_type=jnp.float32
                )
                * score_scale
            )
            old_top, old_total, old_acc = old
            new_top = jnp.maximum(old_top, jnp.max(jnp.where(mask, scores, -1e30), axis=-1))
            raw = jnp.where(mask, jnp.exp(scores - new_top[..., None]), 0.0)
            factor = jnp.exp(old_top - new_top)
            new_total = old_total * factor + jnp.sum(raw, axis=-1)
            added = jnp.einsum(
                "gjqk,kgd->gjqd",
                raw.astype(jnp.bfloat16),
                shard_values,
                preferred_element_type=jnp.float32,
            )
            return (new_top, new_total, old_acc * factor[..., None] + added)

        near = (key_first <= query_pos[-1]) & (key_first + rows_here - 1 >= query_pos[0] - span)
        holds_sink = jnp.any(
            wanted_sink & (sink_pos >= key_first) & (sink_pos < key_first + rows_here)
        )
        return (lax.cond(near | holds_sink, compute, lambda old: old, state), None)

    numbers = jnp.arange(count, dtype=jnp.int32)
    result, unused = lax.scan(one_shard, init, (piece_keys, piece_values, numbers))
    top, total, accum = result
    result = accum / total[..., None]
    return (
        jnp.transpose(result, (2, 0, 1, 3))
        .reshape(rows_here, groups * QPG * HD)
        .astype(jnp.bfloat16)
    )


def solution(mesh):
    in_specs = (P(("ctx", "head"), None), P("ctx", "head"), P("ctx", "head"), P(), P(), P())
    out_specs = P("ctx", "head")
    return jax.shard_map(
        per_device, mesh=mesh, in_specs=in_specs, out_specs=out_specs, check_vma=False
    )
```

profile of v0, /device:TPU:6, one launch (start us, length us, event | category | flops | bytes accessed | tf_op | source)
XLA Modules:
  0.0 430.6 jit_solution(2635686396681601262)
XLA Ops:
  8.0 3.2 copy.27
  11.2 5.3 %all-to-all-start = ((bf16[128,8,1024]{2,0,1:T(8,128)(2,1)}), bf16[128,8,1024]{2,0,1:T(8,128)(2,1)S(1)}, u32[]{:S(2)}, u32[]{:S(2)}) async-start(bf16[128,8,1024]{2,0,1:T(8,128)(2,1)} %bitcast.88), calls=%async_computation | async-start | bytes 4194304 | tf_op jit(solution)/shard_map/all_to_all | solution.py:17
  19.9 23.8 %all-to-all-done = bf16[128,8,1024]{2,0,1:T(8,128)(2,1)S(1)} async-done(((bf16[128,8,1024]{2,0,1:T(8,128)(2,1)}), bf16[128,8,1024]{2,0,1:T(8,128)(2,1)S(1)}, u32[]{:S(2)}, u32[]{:S(2)}) %all-to-all-start) | async-done | bytes 2097184 | tf_op jit(solution)/shard_map/all_to_all | solution.py:17
  44.6 18.6 %all-gather.3.cloned.1.call-done = bf16[16384,128]{1,0:T(8,128)(2,1)} async-done(((bf16[1024,128]{1,0:T(8,128)(2,1)}), bf16[16384,128]{1,0:T(8,128)(2,1)}) %all-gather.3.cloned.1.call-update) | async-done | bytes 4194320 | tf_op jit(solution)/shard_map/all_gather | solution.py:46
  63.2 53.3 %all-gather.5.cloned.1.call-done = bf16[16384,128]{1,0:T(8,128)(2,1)} async-done(((bf16[1024,128]{1,0:T(8,128)(2,1)}), bf16[16384,128]{1,0:T(8,128)(2,1)}) %all-gather.5.cloned.1.call-update) | async-done | bytes 4194320 | tf_op jit(solution)/shard_map/all_gather | solution.py:47
  116.5 2.2 broadcast_in_dim.77
  118.8 298.8 %while.20 = (s32[]{:T(128)}, f32[1,8,1024]{2,1,0:T(8,128)S(1)}, f32[1,8,1024]{2,1,0:T(8,128)S(1)}, f32[1,8,1024,128]{3,2,1,0:T(8,128)}, s32[16]{0:T(128)S(1)}, /...) while((s32[]{:T(128)}, f32[1,8,1024]{2,1,0:T(8,128)S(1)}, ...), condition=%wide.region_10.11_spmd.clone.clone, body=%wide.region_3.10_spmd.clone.clone.sunk | while | flops 4398856704 | bytes 116453032 | solution.py:90
  120.0 1.3 fusion.34
  125.4 1.3 fusion.34
  127.0 0.7 and_reduce_fusion.2
  130.8 1.3 fusion.34
  132.4 0.7 and_reduce_fusion.2
  136.2 1.3 fusion.34
  141.6 1.3 fusion.34
  147.0 1.3 fusion.34
  151.2 53.1 %conditional.4 = ((f32[1,8,1024]{2,1,0:T(8,128)S(1)}, f32[1,8,1024]{2,1,0:T(8,128)S(1)}, f32[1,8,1024,128]{3,2,1,0:T(8,128)})) conditional(s32[]{:T(128)} %convert_element_type.49, (f32[1,8,1024]{2,1,0:T(8,128)S(1)}, f32[1,8,1024]{2,1,0:T(8,128)S(1)}, f32[1,8,1024,128]{3,2,1,0:T(8,128)}) %tuple.67, (s32[]{:T(128)}, s32[1024]{0:T(1024)S(1)}, ...), branch_computations={%region_5.5_spmd, %region_6.9_spmd} | conditional | flops 4398851072 | bytes 116438128 | solution.py:87
  151.3 6.2 %fusion.14 = pred[1024,1024]{0,1:T(8,128)(4,1)S(1)} fusion(s32[]{:T(128)} %bitcast.1, s32[1024]{0:T(1024)S(1)} %get-tuple-element.443, s32[]{:T(128)} %bitcast, s32[1024]{0:T(1024)S(1)} %broadcast_add_fusion.1, s32[1024]{0:T(1024)S(1)} %get-tuple-element.441, s32[1024]{0:T(1024)S(1)} %get-tuple-element.440, s32[1024]{0:T(1024)S(1)} %broadcast_add_fusion), kind=kLoop, calls=%fused_computation.17 | loop fusion | flops 9437184 | bytes 1069064 | tf_op jit(solution)/shard_map/while/body/eval_jaxpr/cond/branch_1_fun/and | solution.py:63
  157.5 14.6 %fusion.4 = (f32[8,1024]{1,0:T(8,128)S(1)}, f32[1024,1024,8]{1,0,2:T(8,128)}) fusion(pred[1024,1024]{0,1:T(8,128)(4,1)S(1)} %fusion.14, bf16[1024,1,8,128]{3,0,2,1:T(8,128)(2,1)S(1)} %get-tuple-element.447, bf16[16,1024,1,128]{3,1,2,0:T(8,128)(2,1)} %get-tuple-element.445, s32[]{:T(128)} %get-tuple-element.446), kind=kOutput, calls=%fused_computation.4 | convolution fusion | flops 2172641280 | bytes 36995584 | tf_op jit(solution)/shard_map/while/body/eval_jaxpr/cond/branch_1_fun/qgjd,kgd->gjqk/dot_general | solution.py:65
  172.1 14.2 %fusion.8 = f32[8,1024]{1,0:T(8,128)S(1)} fusion(f32[1024,1024,8]{1,0,2:T(8,128)} %get-tuple-element.643, f32[8,1024]{1,0:T(8,128)S(1)} %bitcast.85, pred[1024,1024]{0,1:T(8,128)(4,1)S(1)} %fusion.14), kind=kLoop, calls=%fused_computation.8 | loop fusion | flops 33546240 | bytes 34668544 | tf_op jit(solution)/shard_map/while/body/eval_jaxpr/cond/branch_1_fun/reduce_sum | solution.py:74
  186.3 18.0 %bitcast_add_fusion = f32[1,8,1024,128]{3,2,1,0:T(8,128)} fusion(f32[1,8,1024,128]{3,2,1,0:T(8,128)} %get-tuple-element.449, f32[1024,1024,8]{1,0,2:T(8,128)} %get-tuple-element.643, f32[8,1024]{1,0:T(8,128)S(1)} %bitcast.86, pred[1024,1024]{0,1:T(8,128)(4,1)S(1)} %fusion.14, f32[8,1024]{1,0:T(8,128)S(1)} %get-tuple-element.640, ...), kind=kOutput, calls=%fused_computation.14 | convolution fusion | flops 2183135232 | bytes 43319808 | tf_op jit(solution)/shard_map/while/body/eval_jaxpr/cond/branch_1_fun/gjqk,kgd->gjqd/dot_general | solution.py:75
  205.5 1.3 fusion.34
  210.9 1.3 fusion.34
  216.3 1.3 fusion.34
  221.8 1.3 fusion.34
  227.2 1.3 fusion.34
  231.3 53.1 %conditional.4 = ((f32[1,8,1024]{2,1,0:T(8,128)S(1)}, f32[1,8,1024]{2,1,0:T(8,128)S(1)}, f32[1,8,1024,128]{3,2,1,0:T(8,128)})) conditional(s32[]{:T(128)} %convert_element_type.49, (f32[1,8,1024]{2,1,0:T(8,128)S(1)}, f32[1,8,1024]{2,1,0:T(8,128)S(1)}, f32[1,8,1024,128]{3,2,1,0:T(8,128)}) %tuple.67, (s32[]{:T(128)}, s32[1024]{0:T(1024)S(1)}, ...), branch_computations={%region_5.5_spmd, %region_6.9_spmd} | conditional | flops 4398851072 | bytes 116438128 | solution.py:87
  231.4 6.2 %fusion.14 = pred[1024,1024]{0,1:T(8,128)(4,1)S(1)} fusion(s32[]{:T(128)} %bitcast.1, s32[1024]{0:T(1024)S(1)} %get-tuple-element.443, s32[]{:T(128)} %bitcast, s32[1024]{0:T(1024)S(1)} %broadcast_add_fusion.1, s32[1024]{0:T(1024)S(1)} %get-tuple-element.441, s32[1024]{0:T(1024)S(1)} %get-tuple-element.440, s32[1024]{0:T(1024)S(1)} %broadcast_add_fusion), kind=kLoop, calls=%fused_computation.17 | loop fusion | flops 9437184 | bytes 1069064 | tf_op jit(solution)/shard_map/while/body/eval_jaxpr/cond/branch_1_fun/and | solution.py:63
  237.6 14.6 %fusion.4 = (f32[8,1024]{1,0:T(8,128)S(1)}, f32[1024,1024,8]{1,0,2:T(8,128)}) fusion(pred[1024,1024]{0,1:T(8,128)(4,1)S(1)} %fusion.14, bf16[1024,1,8,128]{3,0,2,1:T(8,128)(2,1)S(1)} %get-tuple-element.447, bf16[16,1024,1,128]{3,1,2,0:T(8,128)(2,1)} %get-tuple-element.445, s32[]{:T(128)} %get-tuple-element.446), kind=kOutput, calls=%fused_computation.4 | convolution fusion | flops 2172641280 | bytes 36995584 | tf_op jit(solution)/shard_map/while/body/eval_jaxpr/cond/branch_1_fun/qgjd,kgd->gjqk/dot_general | solution.py:65
  252.2 14.2 %fusion.8 = f32[8,1024]{1,0:T(8,128)S(1)} fusion(f32[1024,1024,8]{1,0,2:T(8,128)} %get-tuple-element.643, f32[8,1024]{1,0:T(8,128)S(1)} %bitcast.85, pred[1024,1024]{0,1:T(8,128)(4,1)S(1)} %fusion.14), kind=kLoop, calls=%fused_computation.8 | loop fusion | flops 33546240 | bytes 34668544 | tf_op jit(solution)/shard_map/while/body/eval_jaxpr/cond/branch_1_fun/reduce_sum | solution.py:74
  266.4 18.0 %bitcast_add_fusion = f32[1,8,1024,128]{3,2,1,0:T(8,128)} fusion(f32[1,8,1024,128]{3,2,1,0:T(8,128)} %get-tuple-element.449, f32[1024,1024,8]{1,0,2:T(8,128)} %get-tuple-element.643, f32[8,1024]{1,0:T(8,128)S(1)} %bitcast.86, pred[1024,1024]{0,1:T(8,128)(4,1)S(1)} %fusion.14, f32[8,1024]{1,0:T(8,128)S(1)} %get-tuple-element.640, ...), kind=kOutput, calls=%fused_computation.14 | convolution fusion | flops 2183135232 | bytes 43319808 | tf_op jit(solution)/shard_map/while/body/eval_jaxpr/cond/branch_1_fun/gjqk,kgd->gjqd/dot_general | solution.py:75
  285.6 1.3 fusion.34
  289.8 53.1 %conditional.4 = ((f32[1,8,1024]{2,1,0:T(8,128)S(1)}, f32[1,8,1024]{2,1,0:T(8,128)S(1)}, f32[1,8,1024,128]{3,2,1,0:T(8,128)})) conditional(s32[]{:T(128)} %convert_element_type.49, (f32[1,8,1024]{2,1,0:T(8,128)S(1)}, f32[1,8,1024]{2,1,0:T(8,128)S(1)}, f32[1,8,1024,128]{3,2,1,0:T(8,128)}) %tuple.67, (s32[]{:T(128)}, s32[1024]{0:T(1024)S(1)}, ...), branch_computations={%region_5.5_spmd, %region_6.9_spmd} | conditional | flops 4398851072 | bytes 116438128 | solution.py:87
  289.9 6.2 %fusion.14 = pred[1024,1024]{0,1:T(8,128)(4,1)S(1)} fusion(s32[]{:T(128)} %bitcast.1, s32[1024]{0:T(1024)S(1)} %get-tuple-element.443, s32[]{:T(128)} %bitcast, s32[1024]{0:T(1024)S(1)} %broadcast_add_fusion.1, s32[1024]{0:T(1024)S(1)} %get-tuple-element.441, s32[1024]{0:T(1024)S(1)} %get-tuple-element.440, s32[1024]{0:T(1024)S(1)} %broadcast_add_fusion), kind=kLoop, calls=%fused_computation.17 | loop fusion | flops 9437184 | bytes 1069064 | tf_op jit(solution)/shard_map/while/body/eval_jaxpr/cond/branch_1_fun/and | solution.py:63
  296.1 14.6 %fusion.4 = (f32[8,1024]{1,0:T(8,128)S(1)}, f32[1024,1024,8]{1,0,2:T(8,128)}) fusion(pred[1024,1024]{0,1:T(8,128)(4,1)S(1)} %fusion.14, bf16[1024,1,8,128]{3,0,2,1:T(8,128)(2,1)S(1)} %get-tuple-element.447, bf16[16,1024,1,128]{3,1,2,0:T(8,128)(2,1)} %get-tuple-element.445, s32[]{:T(128)} %get-tuple-element.446), kind=kOutput, calls=%fused_computation.4 | convolution fusion | flops 2172641280 | bytes 36995584 | tf_op jit(solution)/shard_map/while/body/eval_jaxpr/cond/branch_1_fun/qgjd,kgd->gjqk/dot_general | solution.py:65
  310.7 14.2 %fusion.8 = f32[8,1024]{1,0:T(8,128)S(1)} fusion(f32[1024,1024,8]{1,0,2:T(8,128)} %get-tuple-element.643, f32[8,1024]{1,0:T(8,128)S(1)} %bitcast.85, pred[1024,1024]{0,1:T(8,128)(4,1)S(1)} %fusion.14), kind=kLoop, calls=%fused_computation.8 | loop fusion | flops 33546240 | bytes 34668544 | tf_op jit(solution)/shard_map/while/body/eval_jaxpr/cond/branch_1_fun/reduce_sum | solution.py:74
  324.9 18.0 %bitcast_add_fusion = f32[1,8,1024,128]{3,2,1,0:T(8,128)} fusion(f32[1,8,1024,128]{3,2,1,0:T(8,128)} %get-tuple-element.449, f32[1024,1024,8]{1,0,2:T(8,128)} %get-tuple-element.643, f32[8,1024]{1,0:T(8,128)S(1)} %bitcast.86, pred[1024,1024]{0,1:T(8,128)(4,1)S(1)} %fusion.14, f32[8,1024]{1,0:T(8,128)S(1)} %get-tuple-element.640, ...), kind=kOutput, calls=%fused_computation.14 | convolution fusion | flops 2183135232 | bytes 43319808 | tf_op jit(solution)/shard_map/while/body/eval_jaxpr/cond/branch_1_fun/gjqk,kgd->gjqd/dot_general | solution.py:75
  344.1 1.3 fusion.34
  348.3 53.1 %conditional.4 = ((f32[1,8,1024]{2,1,0:T(8,128)S(1)}, f32[1,8,1024]{2,1,0:T(8,128)S(1)}, f32[1,8,1024,128]{3,2,1,0:T(8,128)})) conditional(s32[]{:T(128)} %convert_element_type.49, (f32[1,8,1024]{2,1,0:T(8,128)S(1)}, f32[1,8,1024]{2,1,0:T(8,128)S(1)}, f32[1,8,1024,128]{3,2,1,0:T(8,128)}) %tuple.67, (s32[]{:T(128)}, s32[1024]{0:T(1024)S(1)}, ...), branch_computations={%region_5.5_spmd, %region_6.9_spmd} | conditional | flops 4398851072 | bytes 116438128 | solution.py:87
  348.4 6.2 %fusion.14 = pred[1024,1024]{0,1:T(8,128)(4,1)S(1)} fusion(s32[]{:T(128)} %bitcast.1, s32[1024]{0:T(1024)S(1)} %get-tuple-element.443, s32[]{:T(128)} %bitcast, s32[1024]{0:T(1024)S(1)} %broadcast_add_fusion.1, s32[1024]{0:T(1024)S(1)} %get-tuple-element.441, s32[1024]{0:T(1024)S(1)} %get-tuple-element.440, s32[1024]{0:T(1024)S(1)} %broadcast_add_fusion), kind=kLoop, calls=%fused_computation.17 | loop fusion | flops 9437184 | bytes 1069064 | tf_op jit(solution)/shard_map/while/body/eval_jaxpr/cond/branch_1_fun/and | solution.py:63
  354.6 14.6 %fusion.4 = (f32[8,1024]{1,0:T(8,128)S(1)}, f32[1024,1024,8]{1,0,2:T(8,128)}) fusion(pred[1024,1024]{0,1:T(8,128)(4,1)S(1)} %fusion.14, bf16[1024,1,8,128]{3,0,2,1:T(8,128)(2,1)S(1)} %get-tuple-element.447, bf16[16,1024,1,128]{3,1,2,0:T(8,128)(2,1)} %get-tuple-element.445, s32[]{:T(128)} %get-tuple-element.446), kind=kOutput, calls=%fused_computation.4 | convolution fusion | flops 2172641280 | bytes 36995584 | tf_op jit(solution)/shard_map/while/body/eval_jaxpr/cond/branch_1_fun/qgjd,kgd->gjqk/dot_general | solution.py:65
  369.2 14.2 %fusion.8 = f32[8,1024]{1,0:T(8,128)S(1)} fusion(f32[1024,1024,8]{1,0,2:T(8,128)} %get-tuple-element.643, f32[8,1024]{1,0:T(8,128)S(1)} %bitcast.85, pred[1024,1024]{0,1:T(8,128)(4,1)S(1)} %fusion.14), kind=kLoop, calls=%fused_computation.8 | loop fusion | flops 33546240 | bytes 34668544 | tf_op jit(solution)/shard_map/while/body/eval_jaxpr/cond/branch_1_fun/reduce_sum | solution.py:74
  383.4 18.0 %bitcast_add_fusion = f32[1,8,1024,128]{3,2,1,0:T(8,128)} fusion(f32[1,8,1024,128]{3,2,1,0:T(8,128)} %get-tuple-element.449, f32[1024,1024,8]{1,0,2:T(8,128)} %get-tuple-element.643, f32[8,1024]{1,0:T(8,128)S(1)} %bitcast.86, pred[1024,1024]{0,1:T(8,128)(4,1)S(1)} %fusion.14, f32[8,1024]{1,0:T(8,128)S(1)} %get-tuple-element.640, ...), kind=kOutput, calls=%fused_computation.14 | convolution fusion | flops 2183135232 | bytes 43319808 | tf_op jit(solution)/shard_map/while/body/eval_jaxpr/cond/branch_1_fun/gjqk,kgd->gjqd/dot_general | solution.py:75
  402.6 1.3 fusion.34
  408.0 1.3 fusion.34
  413.4 1.3 fusion.34
  417.6 2.9 fusion.31
  420.5 1.4 copy.19
  421.8 1.9 copy.26
  (173 shorter events, 38.3 us)
Async XLA Ops:
  6.5 56.7 %all-gather.3.cloned.1.call-start = ((), (), s32[]{:S(2)}) async-start(), calls=%async_computation.1 | async-start | bytes 4456448 | tf_op jit(solution)/shard_map/all_gather | solution.py:46
  7.3 109.3 %all-gather.5.cloned.1.call-start = ((), (), s32[]{:S(2)}) async-start(), calls=%async_computation.2 | async-start | bytes 4456448 | tf_op jit(solution)/shard_map/all_gather | solution.py:47
  8.0 8.5 %copy-start = (s32[16]{0:T(128)S(1)}, s32[16]{0:T(128)}, u32[]{:S(2)}) copy-start(s32[16]{0:T(128)} %param.13) | copy-start | bytes 196
  8.0 8.8 %copy-start.1 = (s32[8]{0:T(128)S(1)}, s32[8]{0:T(128)}, u32[]{:S(2)}) copy-start(s32[8]{0:T(128)} %param.14) | copy-start | bytes 100
  8.0 9.4 %copy-start.2 = (s32[8]{0:T(128)S(1)}, s32[8]{0:T(128)}, u32[]{:S(2)}) copy-start(s32[8]{0:T(128)} %param.15) | copy-start | bytes 100
  11.2 32.5 %all-to-all-start = ((bf16[128,8,1024]{2,0,1:T(8,128)(2,1)}), bf16[128,8,1024]{2,0,1:T(8,128)(2,1)S(1)}, u32[]{:S(2)}, u32[]{:S(2)}) async-start(bf16[128,8,1024]{2,0,1:T(8,128)(2,1)} %bitcast.88), calls=%async_computation | async-start | bytes 4194304 | tf_op jit(solution)/shard_map/all_to_all | solution.py:17
Sparse Core Ops, SparseCore 0:
  9.5 53.6 all-gather.2
  65.4 51.0 all-gather.4
where the time goes:
time: 432 us; the launch traced here: 431 us
  matrix products  130 us (30%)
  other arithmetic  119 us (28%)
  waiting for transfers between devices  97.1 us (22%)
  local copies, waits for them, and re-layouts  33.4 us (8%)
  loops' own time  31.5 us (7%)
  between operations  14.1 us (3%)
  starting transfers between devices  5.35 us (1%)
    dot_general x4, matrix products, compute(): jnp.einsum('gjqk,kgd->gjqd', raw.astype(jnp.bfloat16), shard_values, pref...  71.8 us
    dot_general x4, matrix products, compute(): jnp.einsum('qgjd,kgd->gjqk', queries, shard_keys, preferred_element_type=...  58.3 us
    reduce_sum x4, other arithmetic, compute(): new_total = old_total * factor + jnp.sum(raw, axis=-1)  56.8 us
    all_gather x1, waiting for transfers between devices, per_device(): piece_values = lax.all_gather(value_rows, 'ctx', axis=0, tiled=True)  53.3 us
    another operation x1, loops' own time, per_device(): lax.scan(one_shard, init, (piece_keys, piece_values, numbers))  31.1 us
    and x4, other arithmetic, compute(): mask = (same[None] & (inside | early))[:, None]  24.9 us
    all_to_all x1, waiting for transfers between devices, per_device(): lax.all_to_all(q_rows, 'head', split_axis=1, concat_axis=0, tiled=True)  23.8 us
    and x16, other arithmetic, per_device(): sink_live & (sink_doc >= query_doc[0]) & (sink_doc <= query_doc[-1])  21 us
  transfers between devices with their start and end apart: 3, of which 3 were waited for; matrix products, arithmetic and copies ran while one was open for 2% of the time, Pallas kernels for 0%

commit v1 on v0

v1 whole, which is shorter than its diff:
```python
import functools

import jax
import jax.numpy as jnp
from jax import lax
from jax.experimental import pallas as pl
from jax.experimental.pallas import tpu as pltpu
from jax.sharding import PartitionSpec as P

HD = 128
QPG = 8
WSPAN = 2
SINK_MAX = 32
MESH = pl.DeviceIdType.MESH
EXP2_SCALE = HD ** (-0.5) * 1.4426950408889634
NT = (((1,), (1,)), ((), ()))
HIDDEN = -1e30


def kernel(
    ctx_n, head_n, docs,
    lengths, windows, sinks, q_hbm, k_hbm, v_hbm, out_hbm,
    qbuf, kbuf, vbuf, obuf, bias, ident, first_of, sink_k, sink_v, sink_own, sink_in1, sink_mid, sink_in2,
    q_local, kv_local, q_send, q_recv, kv_send, kv_recv, s1_send, s1_recv, s2_send, s2_recv, o_sem,
):
    ctx = lax.axis_index("ctx")
    head = lax.axis_index("head")
    rows = k_hbm.shape[0]
    chunk = q_hbm.shape[0]
    width = QPG * HD
    near = WSPAN * rows
    reach = near + chunk
    z, core, zn = head // 2, head % 2, head_n // 2
    base = ctx * rows

    def back(d):
        return lax.rem(ctx + d + ctx_n, ctx_n)

    step1 = (1, 2, 3)
    step2 = (1, 5, 9, 13)
    order = [(dz, dc) for dz, dc in ((0, 1), (1, 0), (3, 0), (1, 1), (3, 1), (2, 0), (2, 1))]

    def peer(dz, dc):
        return lax.rem(z + dz, zn) * 2 + lax.rem(core + dc, 2)

    barrier = pltpu.get_barrier_semaphore()
    for d in (13, 9, 5, 3, 2, 1):
        pl.semaphore_signal(barrier, inc=1, device_id=(back(-d), head), device_id_type=MESH)
    for dz, dc in order:
        pl.semaphore_signal(barrier, inc=1, device_id=(ctx, peer(dz, dc)), device_id_type=MESH)

    own_q = pltpu.make_async_copy(
        q_hbm.at[:, pl.ds(pl.multiple_of(head * width, width), width)], qbuf.at[head], q_local
    )
    own_k = pltpu.make_async_copy(k_hbm, kbuf.at[pl.ds(near, rows)], kv_local.at[0])
    own_v = pltpu.make_async_copy(v_hbm, vbuf.at[pl.ds(near, rows)], kv_local.at[1])
    own_k.start()
    own_v.start()
    own_q.start()

    starts = []
    running = jnp.int32(0)
    for d in range(docs):
        starts.append(running)
        running = running + lengths[d]

    def start_of(position):
        found = jnp.int32(-1)
        for s in starts:
            found = jnp.where(position >= s, s, found)
        return found

    window = windows[head]
    sink_width = sinks[head]
    last_doc = {d: start_of(base - d * rows + rows - 1) for d in (0, 1, 2, 3, 5, 9, 13)}
    doc_a = start_of(base)
    doc_b = start_of(base + rows // 2 - 1)
    doc_b = jnp.where(doc_b > base, doc_b, -1)

    iota_r = lax.broadcasted_iota(jnp.int32, (chunk, HD), 0)
    iota_c = lax.broadcasted_iota(jnp.int32, (chunk, HD), 1)
    ident[...] = jnp.where(iota_r == iota_c, 1.0, 0.0).astype(jnp.bfloat16)
    grid_pos = base + lax.broadcasted_iota(jnp.int32, (rows // HD, HD), 0) * HD + lax.broadcasted_iota(
        jnp.int32, (rows // HD, HD), 1
    )
    found = jnp.zeros((rows // HD, HD), jnp.int32)
    for s in starts:
        found = jnp.where(grid_pos >= s, s, found)
    first_of[...] = found
    sink_k[...] = jnp.zeros_like(sink_k)
    sink_v[...] = jnp.zeros_like(sink_v)

    pl.semaphore_wait(barrier, len(order) + 6)

    def q_copy(target, source):
        return pltpu.make_async_remote_copy(
            src_ref=q_hbm.at[:, pl.ds(pl.multiple_of(target * width, width), width)],
            dst_ref=qbuf.at[source],
            send_sem=q_send.at[target],
            recv_sem=q_recv.at[source],
            device_id=(ctx, target),
            device_id_type=MESH,
        )

    def kv_copy(d, which):
        src = (k_hbm, v_hbm)[which]
        dst = (kbuf, vbuf)[which]
        return pltpu.make_async_remote_copy(
            src_ref=src,
            dst_ref=dst.at[pl.ds(near - d * rows, rows)],
            send_sem=kv_send.at[d - 1, which],
            recv_sem=kv_recv.at[d - 1, which],
            device_id=(back(d), head),
            device_id_type=MESH,
        )

    for which in (0, 1):
        kv_copy(1, which).start()
    for dz, dc in order:
        q_copy(peer(dz, dc), head).start()
    for which in (0, 1):
        kv_copy(2, which).start()

    own_k.wait()
    own_v.wait()
    at = base + lax.broadcasted_iota(jnp.int32, (SINK_MAX, rows), 1)
    rank = lax.broadcasted_iota(jnp.int32, (SINK_MAX, rows), 0)
    pick = jnp.concatenate(
        [jnp.where(at == s + rank, 1.0, 0.0).astype(jnp.bfloat16) for s in (last_doc[0], doc_a, doc_b)], axis=0
    )
    own = jnp.concatenate([kbuf[pl.ds(near, rows), :], vbuf[pl.ds(near, rows), :]], axis=1)
    picked = jnp.dot(pick, own, preferred_element_type=jnp.float32).astype(jnp.bfloat16)
    n = SINK_MAX
    sink_own[pl.ds(0, n), :] = picked[:n, :HD]
    sink_own[pl.ds(n, n), :] = picked[:n, HD:]
    sink_k[pl.ds(0, n), :] = picked[n : 2 * n, :HD]
    sink_v[pl.ds(0, n), :] = picked[n : 2 * n, HD:]
    sink_k[pl.ds(n, n), :] = picked[2 * n : 3 * n, :HD]
    sink_v[pl.ds(n, n), :] = picked[2 * n : 3 * n, HD:]

    def s1_copy(j):
        return pltpu.make_async_remote_copy(
            src_ref=sink_own, dst_ref=sink_in1.at[j], send_sem=s1_send.at[j], recv_sem=s1_recv.at[j],
            device_id=(back(step1[j]), head), device_id_type=MESH,
        )

    def s2_copy(j):
        return pltpu.make_async_remote_copy(
            src_ref=sink_mid, dst_ref=sink_in2.at[j], send_sem=s2_send.at[j], recv_sem=s2_recv.at[j],
            device_id=(back(step2[j]), head), device_id_type=MESH,
        )

    for j in range(len(step1)):
        s1_copy(j).start()
    same = lambda a, b: jnp.full((2 * n, HD), a, jnp.int32) == jnp.full((2 * n, HD), b, jnp.int32)
    for j in range(len(step1)):
        s1_copy(j).wait()
    mid = sink_own[...].astype(jnp.float32)
    for j, d in enumerate(step1):
        mid = mid + jnp.where(same(last_doc[d], last_doc[0]), sink_in1[j].astype(jnp.float32), 0.0)
    sink_mid[...] = mid.astype(jnp.bfloat16)
    for j in range(len(step2)):
        s2_copy(j).start()
    for j in range(len(step2)):
        s2_copy(j).wait()
    got = jnp.zeros((2 * n, HD), jnp.float32)
    for j, d in enumerate(step2):
        got = got + jnp.where(same(last_doc[d], doc_a), sink_in2[j].astype(jnp.float32), 0.0)
    sink_k[pl.ds(0, n), :] = (sink_k[pl.ds(0, n), :].astype(jnp.float32) + got[:n]).astype(jnp.bfloat16)
    sink_v[pl.ds(0, n), :] = (sink_v[pl.ds(0, n), :].astype(jnp.float32) + got[n:]).astype(jnp.bfloat16)

    for d in (1, 2):
        for which in (0, 1):
            kv_copy(d, which).wait()
    own_q.wait()

    srank = lax.broadcasted_iota(jnp.int32, (HD, chunk), 0)

    def one_chunk(s, carry):
        dz = jnp.where(s < 2, 0, jnp.where(s < 6, 1 + 2 * (s % 2), 2))
        dc = jnp.where(s < 2, s, jnp.where(s < 6, s // 2 - 1, s - 6))
        i = peer(dz, dc)

        @pl.when(s > 0)
        def _():
            q_copy(i, i).wait()

        lo_row = pl.multiple_of(i * chunk, chunk)
        t = base + i * chunk + lax.broadcasted_iota(jnp.int32, (1, chunk), 1)
        first = first_of[pl.ds(i, 1), :]
        low = jnp.maximum(first, t - window + 1)
        kp = base - near + i * chunk + lax.broadcasted_iota(jnp.int32, (reach, chunk), 0)
        bias[pl.ds(0, reach), :] = jnp.where((kp <= t) & (kp >= low), 0.0, HIDDEN).astype(jnp.bfloat16)
        doc = jnp.where(srank < n, doc_a, jnp.where(srank < 2 * n, doc_b, -1))
        r = srank % n
        seen = (r < sink_width) & (doc == first) & (doc + r <= t - window)
        bias[pl.ds(reach, HD), :] = jnp.where(seen, 0.0, HIDDEN).astype(jnp.bfloat16)

        keys = jnp.concatenate([kbuf[pl.ds(lo_row, reach), :], sink_k[...]], axis=0)
        vals = jnp.concatenate([vbuf[pl.ds(lo_row, reach), :], sink_v[...]], axis=0)
        keys = jnp.concatenate([keys, bias[...]], axis=1)
        vals = jnp.concatenate([vals, jnp.ones((reach + HD, HD), jnp.bfloat16)], axis=1)
        unit = ident[...]
        for h in range(0, QPG, 2):
            left = jnp.concatenate(
                [jnp.concatenate([qbuf[i, :, a * HD : (a + 1) * HD], unit], axis=1) for a in (h, h + 1)], axis=0
            )
            scores = lax.dot_general(left, keys, NT, preferred_element_type=jnp.float32)
            top = jnp.max(scores, axis=1, keepdims=True)
            raw = jnp.exp2(scores * EXP2_SCALE - top * EXP2_SCALE).astype(jnp.bfloat16)
            summed = jnp.dot(raw, vals, preferred_element_type=jnp.float32)
            result = (summed[:, :HD] / summed[:, HD:]).astype(jnp.bfloat16)
            for a in (0, 1):
                obuf[pl.ds(lo_row, chunk), (h + a) * HD : (h + a + 1) * HD] = result[a * chunk : (a + 1) * chunk]
        return carry

    lax.fori_loop(0, head_n, one_chunk, 0)
    result_copy = pltpu.make_async_copy(obuf, out_hbm, o_sem)
    result_copy.start()
    result_copy.wait()


def per_device(ctx_n, head_n, q_rows, key_rows, value_rows, doc_lengths, window_widths, sink_widths):
    rows = key_rows.shape[0]
    chunk = q_rows.shape[0]
    docs = doc_lengths.shape[0]
    span = (WSPAN + 1) * rows
    bf = jnp.bfloat16
    n = SINK_MAX
    dma = pltpu.SemaphoreType.DMA
    return pl.pallas_call(
        functools.partial(kernel, ctx_n, head_n, docs),
        out_shape=jax.ShapeDtypeStruct((rows, QPG * HD), bf),
        in_specs=[pl.BlockSpec(memory_space=pltpu.SMEM)] * 3 + [pl.BlockSpec(memory_space=pl.ANY)] * 3,
        out_specs=pl.BlockSpec(memory_space=pl.ANY),
        scratch_shapes=[
            pltpu.VMEM((head_n, chunk, QPG * HD), bf),
            pltpu.VMEM((span, HD), bf),
            pltpu.VMEM((span, HD), bf),
            pltpu.VMEM((rows, QPG * HD), bf),
            pltpu.VMEM((WSPAN * rows + chunk + HD, chunk), bf),
            pltpu.VMEM((chunk, HD), bf),
            pltpu.VMEM((rows // HD, HD), jnp.int32),
            pltpu.VMEM((HD, HD), bf),
            pltpu.VMEM((HD, HD), bf),
            pltpu.VMEM((2 * n, HD), bf),
            pltpu.VMEM((3, 2 * n, HD), bf),
            pltpu.VMEM((2 * n, HD), bf),
            pltpu.VMEM((4, 2 * n, HD), bf),
            dma,
            dma((2,)),
            dma((head_n,)),
            dma((head_n,)),
            dma((2, 2)),
            dma((2, 2)),
            dma((3,)),
            dma((3,)),
            dma((4,)),
            dma((4,)),
            dma,
        ],
        compiler_params=pltpu.CompilerParams(
            collective_id=0, has_side_effects=True, vmem_limit_bytes=48 * 2**20
        ),
        cost_estimate=pl.CostEstimate(
            flops=4 * rows * QPG * HD * (WSPAN * rows + 2 * chunk),
            bytes_accessed=2 * (2 * rows * QPG * HD + 2 * rows * HD),
            transcendentals=rows * QPG * (WSPAN * rows + 2 * chunk),
        ),
        name="attention",
    )(doc_lengths, window_widths, sink_widths, q_rows, key_rows, value_rows)


def solution(mesh):
    in_specs = (P(("ctx", "head"), None), P("ctx", "head"), P("ctx", "head"), P(), P(), P())
    out_specs = P("ctx", "head")
    return jax.shard_map(
        functools.partial(per_device, mesh.shape["ctx"], mesh.shape["head"]),
        mesh=mesh, in_specs=in_specs, out_specs=out_specs, check_vma=False,
    )
```

time: 432 us -> 85.7 us (0.20)
  the two profiles are of different devices: /device:TPU:6 before, /device:TPU:8 now
where the time goes in v1:
time: 85.7 us; the launch traced here: 85.4 us
  Pallas kernels  78.6 us (92%)
  local copies, waits for them, and re-layouts  6.78 us (8%)
    pallas_call x1, Pallas kernels, per_device(): pl.pallas_call(functools.partial(kernel, ctx_n, head_n, docs), out_shape=...  78.6 us
    unnamed x13, local copies, waits for them, and re-layouts  6.78 us

profile of v1, /device:TPU:8, one launch (start us, length us, event | category | flops | bytes accessed | tf_op | source)
XLA Modules:
  0.0 85.4 jit_solution(14045806558143353374)
XLA Ops:
  0.0 0.0 copy-start
  0.0 1.6 %copy-done = bf16[128,8192]{1,0:T(8,128)(2,1)S(1)} copy-done((bf16[128,8192]{1,0:T(8,128)(2,1)S(1)}, bf16[128,8192]{1,0:T(8,128)(2,1)}, u32[]{:S(2)}) %copy-start) | copy-done | bytes 2097176
  1.6 0.0 copy-start.1
  1.6 0.9 %copy-done.1 = bf16[1024,128]{1,0:T(8,128)(2,1)S(1)} copy-done((bf16[1024,128]{1,0:T(8,128)(2,1)S(1)}, bf16[1024,128]{1,0:T(8,128)(2,1)}, u32[]{:S(2)}) %copy-start.1) | copy-done | bytes 262168
  2.5 0.0 copy-start.2
  2.5 0.9 %copy-done.2 = bf16[1024,128]{1,0:T(8,128)(2,1)S(1)} copy-done((bf16[1024,128]{1,0:T(8,128)(2,1)S(1)}, bf16[1024,128]{1,0:T(8,128)(2,1)}, u32[]{:S(2)}) %copy-start.2) | copy-done | bytes 262168
  3.5 0.0 copy-start.3
  3.5 0.7 copy-done.3
  4.1 0.0 copy-start.4
  4.2 0.7 copy-done.4
  4.8 0.0 copy-start.5
  4.8 0.7 copy-done.5
  5.5 78.6 %attention.1 = bf16[1024,1024]{1,0:T(8,128)(2,1)S(1)} custom-call(s32[16]{0:T(128)S(1)} %copy-done.3, s32[8]{0:T(128)S(1)} %copy-done.4, s32[8]{0:T(128)S(1)} %copy-done.5, bf16[128,8192]{1,0:T(8,128)(2,1)S(1)} %copy-done, bf16[1024,128]{1,0:T(8,128)(2,1)S(1)} %copy-done.1, bf16[1024,128]{1,0:T(8,128)(2,1)S(1)} %copy-done.2), custom_call_target="tpu_custom_call" | custom-call | flops 9663676416 | bytes 4718592 | tf_op jit(solution)/shard_map/attention/pallas_call | solution.py:231
  84.1 1.3 %copy.8 = bf16[1024,1024]{1,0:T(8,128)(2,1)} copy(bf16[1024,1024]{1,0:T(8,128)(2,1)S(1)} %attention.1) | data formatting | bytes 4194304
Async XLA Ops:
  0.0 1.6 %copy-start = (bf16[128,8192]{1,0:T(8,128)(2,1)S(1)}, bf16[128,8192]{1,0:T(8,128)(2,1)}, u32[]{:S(2)}) copy-start(bf16[128,8192]{1,0:T(8,128)(2,1)} %q_hbm.1) | copy-start | bytes 6291460
  1.6 0.9 %copy-start.1 = (bf16[1024,128]{1,0:T(8,128)(2,1)S(1)}, bf16[1024,128]{1,0:T(8,128)(2,1)}, u32[]{:S(2)}) copy-start(bf16[1024,128]{1,0:T(8,128)(2,1)} %k_hbm.1) | copy-start | bytes 786436
  2.5 0.9 %copy-start.2 = (bf16[1024,128]{1,0:T(8,128)(2,1)S(1)}, bf16[1024,128]{1,0:T(8,128)(2,1)}, u32[]{:S(2)}) copy-start(bf16[1024,128]{1,0:T(8,128)(2,1)} %v_hbm.1) | copy-start | bytes 786436
  3.5 0.7 copy-start.3
  4.1 0.7 copy-start.4
  4.8 0.7 copy-start.5

commit v2 on v1

v2 whole, which is shorter than its diff:
```python
import functools

import jax
import jax.numpy as jnp
from jax import lax
from jax.experimental import pallas as pl
from jax.experimental.pallas import tpu as pltpu
from jax.sharding import PartitionSpec as P

HD = 128
QPG = 8
WSPAN = 2
SINK_MAX = 32
MESH = pl.DeviceIdType.MESH
EXP2_SCALE = HD ** (-0.5) * 1.4426950408889634
NT = (((1,), (1,)), ((), ()))
HIDDEN = -1e30


def kernel(
    ctx_n, head_n, docs,
    lengths_hbm, windows_hbm, sinks_hbm, q_hbm, k_hbm, v_hbm, out_hbm,
    qbuf, kbuf, vbuf, obuf, held, bias, ident, first_of, sink_k, sink_v, sink_own, sink_in1, sink_mid, sink_in2,
    relay, acc, tops, lengths, windows, sinks,
    small_local, q_local, kv_local, q_send, q_recv, kv_send, kv_recv, relay_send, relay_recv,
    s1_send, s1_recv, s2_send, s2_recv, o_sem,
):
    ctx = lax.axis_index("ctx")
    head = lax.axis_index("head")
    rows = k_hbm.shape[0]
    chunk = q_hbm.shape[0]
    width = QPG * HD
    near = WSPAN * rows
    z, core, zn = head // 2, head % 2, head_n // 2
    base = ctx * rows

    def back_of(c):
        return lax.rem(c + ctx_n, ctx_n)

    def back(d):
        return back_of(ctx + d)

    step1 = (1, 2, 3)
    step2 = (1, 5, 9, 13)
    order = [(dz, dc) for dz, dc in ((0, 1), (1, 0), (3, 0), (1, 1), (3, 1), (2, 0), (2, 1))]

    y_n = 4
    x, y = ctx // y_n, ctx % y_n
    below = x * y_n + lax.rem(y + y_n - 1, y_n)
    above = x * y_n + lax.rem(y + 1, y_n)
    relay_to = back_of(above + 2)
    two_back = back_of(ctx - 2)
    relay_from = two_back // y_n * y_n + lax.rem(two_back + y_n - 1, y_n)

    def peer(dz, dc):
        return lax.rem(z + dz, zn) * 2 + lax.rem(core + dc, 2)

    barrier = pltpu.get_barrier_semaphore()
    for d in (13, 9, 5, 3, 2, 1):
        pl.semaphore_signal(barrier, inc=1, device_id=(back(-d), head), device_id_type=MESH)
    for c in (relay_from, above):
        pl.semaphore_signal(barrier, inc=1, device_id=(c, head), device_id_type=MESH)
    for dz, dc in order:
        pl.semaphore_signal(barrier, inc=1, device_id=(ctx, peer(dz, dc)), device_id_type=MESH)

    own_q = pltpu.make_async_copy(
        q_hbm.at[:, pl.ds(pl.multiple_of(head * width, width), width)], qbuf.at[head], q_local
    )
    own_k = pltpu.make_async_copy(k_hbm, kbuf.at[pl.ds(near, rows)], kv_local.at[0])
    own_v = pltpu.make_async_copy(v_hbm, vbuf.at[pl.ds(near, rows)], kv_local.at[1])
    small = [
        pltpu.make_async_copy(src, dst, small_local.at[j])
        for j, (src, dst) in enumerate(((lengths_hbm, lengths), (windows_hbm, windows), (sinks_hbm, sinks)))
    ]
    for copy in small:
        copy.start()
    own_k.start()
    own_v.start()
    own_q.start()
    for copy in small:
        copy.wait()

    starts = []
    running = jnp.int32(0)
    for d in range(docs):
        starts.append(running)
        running = running + lengths[d]

    def start_of(position):
        found = jnp.int32(-1)
        for s in starts:
            found = jnp.where(position >= s, s, found)
        return found

    window = windows[head]
    sink_width = sinks[head]
    last_doc = {d: start_of(base - d * rows + rows - 1) for d in (0, 1, 2, 3, 5, 9, 13)}
    doc_a = start_of(base)
    doc_b = start_of(base + rows // 2 - 1)
    doc_b = jnp.where(doc_b > base, doc_b, -1)

    iota_r = lax.broadcasted_iota(jnp.int32, (chunk, HD), 0)
    iota_c = lax.broadcasted_iota(jnp.int32, (chunk, HD), 1)
    ident[...] = jnp.where(iota_r == iota_c, 1.0, 0.0).astype(jnp.bfloat16)
    grid_pos = base + lax.broadcasted_iota(jnp.int32, (rows // HD, HD), 0) * HD + lax.broadcasted_iota(
        jnp.int32, (rows // HD, HD), 1
    )
    found = jnp.zeros((rows // HD, HD), jnp.int32)
    for s in starts:
        found = jnp.where(grid_pos >= s, s, found)
    first_of[...] = found
    sink_k[...] = jnp.zeros_like(sink_k)
    sink_v[...] = jnp.zeros_like(sink_v)

    n = SINK_MAX
    srank = lax.broadcasted_iota(jnp.int32, (HD, chunk), 0)

    def place(s):
        dz = jnp.where(s < 2, 0, jnp.where(s < 6, 1 + 2 * (s % 2), 2))
        dc = jnp.where(s < 2, s, jnp.where(s < 6, s // 2 - 1, s - 6))
        return peer(dz, dc)

    def limits(i):
        t = base + i * chunk + lax.broadcasted_iota(jnp.int32, (1, chunk), 1)
        first = first_of[pl.ds(i, 1), :]
        return t, first, jnp.maximum(first, t - window + 1)

    def set_sink_bias(slot, at, t, first):
        doc = jnp.where(srank < n, doc_a, jnp.where(srank < 2 * n, doc_b, -1))
        r = srank % n
        seen = (r < sink_width) & (doc == first) & (doc + r <= t - window)
        bias[slot, pl.ds(at, HD), :] = jnp.where(seen, 0.0, HIDDEN).astype(jnp.bfloat16)

    def pipeline(lo, hi, reach, row_of, with_sinks, stage, wait_queries):
        total = reach + (HD if with_sinks else 0)

        def set_bias(i, slot):
            t, first, low = limits(i)
            kp = base - near + row_of(i) + lax.broadcasted_iota(jnp.int32, (reach, chunk), 0)
            bias[slot, pl.ds(0, reach), :] = jnp.where((kp <= t) & (kp >= low), 0.0, HIDDEN).astype(jnp.bfloat16)
            if with_sinks:
                set_sink_bias(slot, reach, t, first)

        def score(i, slot, h):
            keys = kbuf[pl.ds(row_of(i), reach), :]
            if with_sinks:
                keys = jnp.concatenate([keys, sink_k[...]], axis=0)
            keys = jnp.concatenate([keys, bias[slot, pl.ds(0, total), :]], axis=1)
            unit = ident[...]
            left = jnp.concatenate(
                [jnp.concatenate([qbuf[i, :, a * HD : (a + 1) * HD], unit], axis=1) for a in (h, h + 1)], axis=0
            )
            return lax.dot_general(left, keys, NT, preferred_element_type=jnp.float32)

        def finish(s, i, h, scores):
            vals = vbuf[pl.ds(row_of(i), reach), :]
            if with_sinks:
                vals = jnp.concatenate([vals, sink_v[...]], axis=0)
            vals = jnp.concatenate([vals, jnp.ones((total, HD), jnp.bfloat16)], axis=1)
            span = pl.ds(h * chunk, 2 * chunk)
            top = jnp.max(scores, axis=1, keepdims=True)
            if stage == "last":
                old = tops[s, span, :]
                top = jnp.maximum(old[:, :1], top)
            raw = jnp.exp2(scores * EXP2_SCALE - top * EXP2_SCALE).astype(jnp.bfloat16)
            summed = jnp.dot(raw, vals, preferred_element_type=jnp.float32)
            if stage == "first":
                tops[s, span, :] = jnp.broadcast_to(top, (2 * chunk, HD))
                acc[s, span, :] = summed
                return
            if stage == "last":
                factor = jnp.exp2(old * EXP2_SCALE - jnp.broadcast_to(top * EXP2_SCALE, (2 * chunk, HD)))
                summed = summed + acc[s, span, :] * jnp.concatenate([factor, factor], axis=1)
            result = (summed[:, :HD] / summed[:, HD:]).astype(jnp.bfloat16)
            for a in (0, 1):
                obuf[pl.ds(pl.multiple_of(i * chunk, chunk), chunk), (h + a) * HD : (h + a + 1) * HD] = result[
                    a * chunk : (a + 1) * chunk
                ]

        def body(s, carry):
            slot = lax.rem(s - lo, 2)
            later = jnp.where(s + 1 < hi, s + 1, s)
            i, j = place(s), place(later)
            if wait_queries:

                @pl.when(s + 1 < hi)
                def _():
                    q_copy(j, j).wait()

            set_bias(j, 1 - slot)
            scores = held[:, pl.ds(0, total)]
            for h in range(0, QPG, 2):
                ahead = score(i, slot, h + 2) if h + 2 < QPG else score(j, 1 - slot, 0)
                finish(s, i, h, scores)
                scores = ahead
            held[:, pl.ds(0, total)] = scores
            if stage != "first":
                o_copy(i).start()
            return carry

        i = place(lo)
        if wait_queries and lo > 0:
            q_copy(i, i).wait()
        set_bias(i, 0)
        held[:, pl.ds(0, total)] = score(i, 0, 0)
        lax.fori_loop(lo, hi, body, 0)

    def o_copy(i):
        span = pl.ds(pl.multiple_of(i * chunk, chunk), chunk)
        return pltpu.make_async_copy(obuf.at[span], out_hbm.at[span], o_sem.at[i])

    own_k.wait()
    own_v.wait()
    at = base + lax.broadcasted_iota(jnp.int32, (SINK_MAX, rows), 1)
    rank = lax.broadcasted_iota(jnp.int32, (SINK_MAX, rows), 0)
    pick = jnp.concatenate(
        [jnp.where(at == s + rank, 1.0, 0.0).astype(jnp.bfloat16) for s in (last_doc[0], doc_a, doc_b)], axis=0
    )
    own = jnp.concatenate([kbuf[pl.ds(near, rows), :], vbuf[pl.ds(near, rows), :]], axis=1)
    picked = jnp.dot(pick, own, preferred_element_type=jnp.float32).astype(jnp.bfloat16)
    sink_own[pl.ds(0, n), :] = picked[:n, :HD]
    sink_own[pl.ds(n, n), :] = picked[:n, HD:]
    sink_k[pl.ds(0, n), :] = picked[n : 2 * n, :HD]
    sink_v[pl.ds(0, n), :] = picked[n : 2 * n, HD:]
    sink_k[pl.ds(n, n), :] = picked[2 * n : 3 * n, :HD]
    sink_v[pl.ds(n, n), :] = picked[2 * n : 3 * n, HD:]

    pl.semaphore_wait(barrier, len(order) + 8)

    def q_copy(target, source):
        return pltpu.make_async_remote_copy(
            src_ref=q_hbm.at[:, pl.ds(pl.multiple_of(target * width, width), width)],
            dst_ref=qbuf.at[source],
            send_sem=q_send.at[target],
            recv_sem=q_recv.at[source],
            device_id=(ctx, target),
            device_id_type=MESH,
        )

    def kv_copy(d, which):
        src = (k_hbm, v_hbm)[which]
        dst = (kbuf, vbuf)[which]
        return pltpu.make_async_remote_copy(
            src_ref=src,
            dst_ref=dst.at[pl.ds(near - d * rows, rows)],
            send_sem=kv_send.at[d - 1, which],
            recv_sem=kv_recv.at[d - 1, which],
            device_id=(back(d), head),
            device_id_type=MESH,
        )

    hop1 = pltpu.make_async_remote_copy(
        src_ref=v_hbm, dst_ref=relay, send_sem=relay_send.at[0], recv_sem=relay_recv,
        device_id=(below, head), device_id_type=MESH,
    )
    hop2 = pltpu.make_async_remote_copy(
        src_ref=relay, dst_ref=vbuf.at[pl.ds(0, rows)], send_sem=relay_send.at[1], recv_sem=kv_recv.at[1, 1],
        device_id=(relay_to, head), device_id_type=MESH,
    )
    def s1_copy(j):
        return pltpu.make_async_remote_copy(
            src_ref=sink_own, dst_ref=sink_in1.at[j], send_sem=s1_send.at[j], recv_sem=s1_recv.at[j],
            device_id=(back(step1[j]), head), device_id_type=MESH,
        )

    def s2_copy(j):
        return pltpu.make_async_remote_copy(
            src_ref=sink_mid, dst_ref=sink_in2.at[j], send_sem=s2_send.at[j], recv_sem=s2_recv.at[j],
            device_id=(back(step2[j]), head), device_id_type=MESH,
        )

    for j in range(len(step1)):
        s1_copy(j).start()
    for which in (0, 1):
        kv_copy(1, which).start()
    hop1.start()
    for dz, dc in order:
        q_copy(peer(dz, dc), head).start()


    same = lambda a, b: jnp.full((2 * n, HD), a, jnp.int32) == jnp.full((2 * n, HD), b, jnp.int32)
    for j in range(len(step1)):
        s1_copy(j).wait()
    mid = sink_own[...].astype(jnp.float32)
    for j, d in enumerate(step1):
        mid = mid + jnp.where(same(last_doc[d], last_doc[0]), sink_in1[j].astype(jnp.float32), 0.0)
    sink_mid[...] = mid.astype(jnp.bfloat16)
    for j in range(len(step2)):
        s2_copy(j).start()
    hop1.wait()
    hop2.start()
    for which in (0, 1):
        kv_copy(1, which).wait()
    kv_copy(2, 0).start()
    own_q.wait()
    early = 4
    recent = rows - chunk
    pipeline(
        0, early, rows, lambda i: pl.multiple_of(near - recent + i * chunk, chunk), False, "first", True
    )
    for j in range(len(step2)):
        s2_copy(j).wait()
    got = jnp.zeros((2 * n, HD), jnp.float32)
    for j, d in enumerate(step2):
        got = got + jnp.where(same(last_doc[d], doc_a), sink_in2[j].astype(jnp.float32), 0.0)
    sink_k[pl.ds(0, n), :] = (sink_k[pl.ds(0, n), :].astype(jnp.float32) + got[:n]).astype(jnp.bfloat16)
    sink_v[pl.ds(0, n), :] = (sink_v[pl.ds(0, n), :].astype(jnp.float32) + got[n:]).astype(jnp.bfloat16)

    kv_copy(2, 0).wait()
    hop2.wait()
    pipeline(0, early, near - recent, lambda i: pl.multiple_of(i * chunk, chunk), True, "last", False)
    pipeline(early, head_n, near + chunk, lambda i: pl.multiple_of(i * chunk, chunk), True, "only", True)
    for i in range(head_n):
        o_copy(i).wait()


def per_device(ctx_n, head_n, q_rows, key_rows, value_rows, doc_lengths, window_widths, sink_widths):
    rows = key_rows.shape[0]
    chunk = q_rows.shape[0]
    docs = doc_lengths.shape[0]
    span = (WSPAN + 1) * rows
    bf = jnp.bfloat16
    n = SINK_MAX
    dma = pltpu.SemaphoreType.DMA
    return pl.pallas_call(
        functools.partial(kernel, ctx_n, head_n, docs),
        out_shape=jax.ShapeDtypeStruct((rows, QPG * HD), bf),
        in_specs=[pl.BlockSpec(memory_space=pltpu.HBM)] * 6,
        out_specs=pl.BlockSpec(memory_space=pltpu.HBM),
        scratch_shapes=[
            pltpu.VMEM((head_n, chunk, QPG * HD), bf),
            pltpu.VMEM((span, HD), bf),
            pltpu.VMEM((span, HD), bf),
            pltpu.VMEM((rows, QPG * HD), bf),
            pltpu.VMEM((2 * chunk, WSPAN * rows + chunk + HD), jnp.float32),
            pltpu.VMEM((2, WSPAN * rows + chunk + HD, chunk), bf),
            pltpu.VMEM((chunk, HD), bf),
            pltpu.VMEM((rows // HD, HD), jnp.int32),
            pltpu.VMEM((HD, HD), bf),
            pltpu.VMEM((HD, HD), bf),
            pltpu.VMEM((2 * n, HD), bf),
            pltpu.VMEM((3, 2 * n, HD), bf),
            pltpu.VMEM((2 * n, HD), bf),
            pltpu.VMEM((4, 2 * n, HD), bf),
            pltpu.VMEM((rows, HD), bf),
            pltpu.VMEM((4, chunk * QPG, 2 * HD), jnp.float32),
            pltpu.VMEM((4, chunk * QPG, HD), jnp.float32),
            pltpu.SMEM(doc_lengths.shape, jnp.int32),
            pltpu.SMEM(window_widths.shape, jnp.int32),
            pltpu.SMEM(sink_widths.shape, jnp.int32),
            dma((3,)),
            dma,
            dma((2,)),
            dma((head_n,)),
            dma((head_n,)),
            dma((2, 2)),
            dma((2, 2)),
            dma((2,)),
            dma,
            dma((3,)),
            dma((3,)),
            dma((4,)),
            dma((4,)),
            dma((head_n,)),
        ],
        compiler_params=pltpu.CompilerParams(
            collective_id=0, has_side_effects=True, vmem_limit_bytes=48 * 2**20
        ),
        cost_estimate=pl.CostEstimate(
            flops=4 * rows * QPG * HD * (WSPAN * rows + 2 * chunk),
            bytes_accessed=2 * (2 * rows * QPG * HD + 2 * rows * HD),
            transcendentals=rows * QPG * (WSPAN * rows + 2 * chunk),
        ),
        name="attention",
    )(doc_lengths, window_widths, sink_widths, q_rows, key_rows, value_rows)


def solution(mesh):
    in_specs = (P(("ctx", "head"), None), P("ctx", "head"), P("ctx", "head"), P(), P(), P())
    out_specs = P("ctx", "head")
    return jax.shard_map(
        functools.partial(per_device, mesh.shape["ctx"], mesh.shape["head"]),
        mesh=mesh, in_specs=in_specs, out_specs=out_specs, check_vma=False,
    )
```

time: 85.7 us -> 60.3 us (0.70)
  the two profiles are of different devices: /device:TPU:8 before, /device:TPU:0 now
where the time goes in v2:
time: 60.3 us; the launch traced here: 60.1 us
  Pallas kernels  53.3 us (88%)
  local copies, waits for them, and re-layouts  6.78 us (11%)
    pallas_call x1, Pallas kernels, per_device(): pl.pallas_call(functools.partial(kernel, ctx_n, head_n, docs), out_shape=...  53.3 us
    unnamed x13, local copies, waits for them, and re-layouts  6.78 us

profile of v2, /device:TPU:0, one launch (start us, length us, event | category | flops | bytes accessed | tf_op | source)
XLA Modules:
  0.0 60.1 jit_solution(9175832544563804349)
XLA Ops:
  0.0 0.0 copy-start
  0.0 1.6 %copy-done = bf16[128,8192]{1,0:T(8,128)(2,1)S(1)} copy-done((bf16[128,8192]{1,0:T(8,128)(2,1)S(1)}, bf16[128,8192]{1,0:T(8,128)(2,1)}, u32[]{:S(2)}) %copy-start) | copy-done | bytes 2097176
  1.6 0.0 copy-start.1
  1.6 0.9 %copy-done.1 = bf16[1024,128]{1,0:T(8,128)(2,1)S(1)} copy-done((bf16[1024,128]{1,0:T(8,128)(2,1)S(1)}, bf16[1024,128]{1,0:T(8,128)(2,1)}, u32[]{:S(2)}) %copy-start.1) | copy-done | bytes 262168
  2.5 0.0 copy-start.2
  2.5 0.9 %copy-done.2 = bf16[1024,128]{1,0:T(8,128)(2,1)S(1)} copy-done((bf16[1024,128]{1,0:T(8,128)(2,1)S(1)}, bf16[1024,128]{1,0:T(8,128)(2,1)}, u32[]{:S(2)}) %copy-start.2) | copy-done | bytes 262168
  3.5 0.0 copy-start.3
  3.5 0.7 %copy-done.3 = s32[16]{0:T(128)S(1)} copy-done((s32[16]{0:T(128)S(1)}, s32[16]{0:T(128)}, u32[]{:S(2)}) %copy-start.3) | copy-done | bytes 88
  4.1 0.0 copy-start.4
  4.2 0.7 %copy-done.4 = s32[8]{0:T(128)S(1)} copy-done((s32[8]{0:T(128)S(1)}, s32[8]{0:T(128)}, u32[]{:S(2)}) %copy-start.4) | copy-done | bytes 56
  4.8 0.0 copy-start.5
  4.8 0.7 %copy-done.5 = s32[8]{0:T(128)S(1)} copy-done((s32[8]{0:T(128)S(1)}, s32[8]{0:T(128)}, u32[]{:S(2)}) %copy-start.5) | copy-done | bytes 56
  5.5 53.3 %attention.1 = bf16[1024,1024]{1,0:T(8,128)(2,1)S(1)} custom-call(s32[16]{0:T(128)S(1)} %copy-done.3, s32[8]{0:T(128)S(1)} %copy-done.4, s32[8]{0:T(128)S(1)} %copy-done.5, bf16[128,8192]{1,0:T(8,128)(2,1)S(1)} %copy-done, bf16[1024,128]{1,0:T(8,128)(2,1)S(1)} %copy-done.1, bf16[1024,128]{1,0:T(8,128)(2,1)S(1)} %copy-done.2), custom_call_target="tpu_custom_call" | custom-call | flops 9663676416 | bytes 4718592 | tf_op jit(solution)/shard_map/attention/pallas_call | solution.py:325
  58.8 1.3 %copy.8 = bf16[1024,1024]{1,0:T(8,128)(2,1)} copy(bf16[1024,1024]{1,0:T(8,128)(2,1)S(1)} %attention.1) | data formatting | bytes 4194304
Async XLA Ops:
  0.0 1.6 %copy-start = (bf16[128,8192]{1,0:T(8,128)(2,1)S(1)}, bf16[128,8192]{1,0:T(8,128)(2,1)}, u32[]{:S(2)}) copy-start(bf16[128,8192]{1,0:T(8,128)(2,1)} %q_hbm.1) | copy-start | bytes 6291460
  1.6 0.9 %copy-start.1 = (bf16[1024,128]{1,0:T(8,128)(2,1)S(1)}, bf16[1024,128]{1,0:T(8,128)(2,1)}, u32[]{:S(2)}) copy-start(bf16[1024,128]{1,0:T(8,128)(2,1)} %k_hbm.1) | copy-start | bytes 786436
  2.5 0.9 %copy-start.2 = (bf16[1024,128]{1,0:T(8,128)(2,1)S(1)}, bf16[1024,128]{1,0:T(8,128)(2,1)}, u32[]{:S(2)}) copy-start(bf16[1024,128]{1,0:T(8,128)(2,1)} %v_hbm.1) | copy-start | bytes 786436
  3.5 0.7 %copy-start.3 = (s32[16]{0:T(128)S(1)}, s32[16]{0:T(128)}, u32[]{:S(2)}) copy-start(s32[16]{0:T(128)} %lengths_hbm.1) | copy-start | bytes 196
  4.1 0.7 %copy-start.4 = (s32[8]{0:T(128)S(1)}, s32[8]{0:T(128)}, u32[]{:S(2)}) copy-start(s32[8]{0:T(128)} %windows_hbm.1) | copy-start | bytes 100
  4.8 0.7 %copy-start.5 = (s32[8]{0:T(128)S(1)}, s32[8]{0:T(128)}, u32[]{:S(2)}) copy-start(s32[8]{0:T(128)} %sinks_hbm.1) | copy-start | bytes 100

commit v3 on v2

--- a/solution.py
+++ b/solution.py
@@ -20,7 +20,7 @@
 def kernel(
     ctx_n, head_n, docs,
     lengths_hbm, windows_hbm, sinks_hbm, q_hbm, k_hbm, v_hbm, out_hbm,
-    qbuf, kbuf, vbuf, obuf, held, bias, ident, first_of, sink_k, sink_v, sink_own, sink_in1, sink_mid, sink_in2,
+    qbuf, kbuf, vbuf, obuf, held, bias, ident, first_of, sink_k, sink_v, sink_own, sink_in1, sink_sum, sink_mid, sink_in2,
     relay, acc, tops, lengths, windows, sinks,
     small_local, q_local, kv_local, q_send, q_recv, kv_send, kv_recv, relay_send, relay_recv,
     s1_send, s1_recv, s2_send, s2_recv, o_sem,
@@ -40,26 +40,31 @@
     def back(d):
         return back_of(ctx + d)
 
-    step1 = (1, 2, 3)
-    step2 = (1, 5, 9, 13)
+    step1 = (1, 2, 3, 4)
+    stride = 4
+    step2 = (4, 8, 12)
     order = [(dz, dc) for dz, dc in ((0, 1), (1, 0), (3, 0), (1, 1), (3, 1), (2, 0), (2, 1))]
 
-    y_n = 4
-    x, y = ctx // y_n, ctx % y_n
-    below = x * y_n + lax.rem(y + y_n - 1, y_n)
-    above = x * y_n + lax.rem(y + 1, y_n)
-    relay_to = back_of(above + 2)
+    x, y = ctx // stride, ctx % stride
+    below = x * stride + lax.rem(y + stride - 1, stride)
+    above = x * stride + lax.rem(y + 1, stride)
     two_back = back_of(ctx - 2)
-    relay_from = two_back // y_n * y_n + lax.rem(two_back + y_n - 1, y_n)
+    relay_from = two_back // stride * stride + lax.rem(two_back + stride - 1, stride)
+    last = ctx_n - 1
 
     def peer(dz, dc):
         return lax.rem(z + dz, zn) * 2 + lax.rem(core + dc, 2)
 
     barrier = pltpu.get_barrier_semaphore()
-    for d in (13, 9, 5, 3, 2, 1):
-        pl.semaphore_signal(barrier, inc=1, device_id=(back(-d), head), device_id_type=MESH)
-    for c in (relay_from, above):
+    def greet(c):
         pl.semaphore_signal(barrier, inc=1, device_id=(c, head), device_id_type=MESH)
+
+    for d in step1 + step2[1:]:
+        pl.when(ctx >= d)(functools.partial(greet, back(-d)))
+    pl.when(ctx >= 2)(functools.partial(greet, relay_from))
+    pl.when(above + 2 <= last)(functools.partial(greet, above))
+    to_ctx = jnp.minimum(last - ctx, len(step1)) + sum(jnp.where(ctx + d <= last, 1, 0) for d in step2[1:])
+    to_ctx = to_ctx + jnp.where(ctx + 2 <= last, 1, 0) + jnp.where(above + 2 <= last, 1, 0)
     for dz, dc in order:
         pl.semaphore_signal(barrier, inc=1, device_id=(ctx, peer(dz, dc)), device_id_type=MESH)
 
@@ -94,7 +99,8 @@
 
     window = windows[head]
     sink_width = sinks[head]
-    last_doc = {d: start_of(base - d * rows + rows - 1) for d in (0, 1, 2, 3, 5, 9, 13)}
+    last_doc = {d: start_of(base - d * rows + rows - 1) for d in (0,) + step1}
+    doc_before = {d: start_of(base - d * rows) for d in step2}
     doc_a = start_of(base)
     doc_b = start_of(base + rows // 2 - 1)
     doc_b = jnp.where(doc_b > base, doc_b, -1)
@@ -109,6 +115,16 @@
     for s in starts:
         found = jnp.where(grid_pos >= s, s, found)
     first_of[...] = found
+    @pl.when(ctx == 0)
+    def _():
+        kbuf[pl.ds(rows, rows), :] = jnp.zeros((rows, HD), jnp.bfloat16)
+        vbuf[pl.ds(rows, rows), :] = jnp.zeros((rows, HD), jnp.bfloat16)
+
+    @pl.when(ctx < 2)
+    def _():
+        kbuf[pl.ds(0, rows), :] = jnp.zeros((rows, HD), jnp.bfloat16)
+        vbuf[pl.ds(0, rows), :] = jnp.zeros((rows, HD), jnp.bfloat16)
+
     sink_k[...] = jnp.zeros_like(sink_k)
     sink_v[...] = jnp.zeros_like(sink_v)
 
@@ -131,7 +147,7 @@
         seen = (r < sink_width) & (doc == first) & (doc + r <= t - window)
         bias[slot, pl.ds(at, HD), :] = jnp.where(seen, 0.0, HIDDEN).astype(jnp.bfloat16)
 
-    def pipeline(lo, hi, reach, row_of, with_sinks, stage, wait_queries):
+    def pipeline(lo, hi, reach, row_of, with_sinks, stage, wait_queries, on_the_way=()):
         total = reach + (HD if with_sinks else 0)
 
         def set_bias(i, slot):
@@ -181,11 +197,13 @@
             slot = lax.rem(s - lo, 2)
             later = jnp.where(s + 1 < hi, s + 1, s)
             i, j = place(s), place(later)
+            for k, action in enumerate(on_the_way):
+                pl.when(s == lo + k)(action)
             if wait_queries:
 
                 @pl.when(s + 1 < hi)
                 def _():
-                    q_copy(j, j).wait()
+                    q_copy(j, j).wait_recv()
 
             set_bias(j, 1 - slot)
             scores = held[:, pl.ds(0, total)]
@@ -200,7 +218,7 @@
 
         i = place(lo)
         if wait_queries and lo > 0:
-            q_copy(i, i).wait()
+            q_copy(i, i).wait_recv()
         set_bias(i, 0)
         held[:, pl.ds(0, total)] = score(i, 0, 0)
         lax.fori_loop(lo, hi, body, 0)
@@ -225,7 +243,7 @@
     sink_k[pl.ds(n, n), :] = picked[2 * n : 3 * n, :HD]
     sink_v[pl.ds(n, n), :] = picked[2 * n : 3 * n, HD:]
 
-    pl.semaphore_wait(barrier, len(order) + 8)
+    pl.semaphore_wait(barrier, len(order) + to_ctx)
 
     def q_copy(target, source):
         return pltpu.make_async_remote_copy(
@@ -237,30 +255,40 @@
             device_id_type=MESH,
         )
 
-    def kv_copy(d, which):
+    cut = 3 * chunk
+
+    def kv_copy(d, which, lo, count, sem):
         src = (k_hbm, v_hbm)[which]
         dst = (kbuf, vbuf)[which]
         return pltpu.make_async_remote_copy(
-            src_ref=src,
-            dst_ref=dst.at[pl.ds(near - d * rows, rows)],
-            send_sem=kv_send.at[d - 1, which],
-            recv_sem=kv_recv.at[d - 1, which],
+            src_ref=src.at[pl.ds(lo, count)],
+            dst_ref=dst.at[pl.ds(near - d * rows + lo, count)],
+            send_sem=kv_send.at[sem, which],
+            recv_sem=kv_recv.at[sem, which],
             device_id=(back(d), head),
             device_id_type=MESH,
         )
 
+    def late_rows(which):
+        return kv_copy(1, which, cut, rows - cut, 0)
+
+    def early_rows(which):
+        return kv_copy(1, which, 0, cut, 2)
+
+    far_keys = kv_copy(2, 0, 0, rows, 1)
+
     hop1 = pltpu.make_async_remote_copy(
         src_ref=v_hbm, dst_ref=relay, send_sem=relay_send.at[0], recv_sem=relay_recv,
         device_id=(below, head), device_id_type=MESH,
     )
     hop2 = pltpu.make_async_remote_copy(
         src_ref=relay, dst_ref=vbuf.at[pl.ds(0, rows)], send_sem=relay_send.at[1], recv_sem=kv_recv.at[1, 1],
-        device_id=(relay_to, head), device_id_type=MESH,
-    )
-    def s1_copy(j):
+        device_id=(back_of(above + 2), head), device_id_type=MESH,
+    )
+    def s1_copy(d):
         return pltpu.make_async_remote_copy(
-            src_ref=sink_own, dst_ref=sink_in1.at[j], send_sem=s1_send.at[j], recv_sem=s1_recv.at[j],
-            device_id=(back(step1[j]), head), device_id_type=MESH,
+            src_ref=sink_own, dst_ref=sink_in1.at[d - 1], send_sem=s1_send.at[d - 1], recv_sem=s1_recv.at[d - 1],
+            device_id=(back(d), head), device_id_type=MESH,
         )
 
     def s2_copy(j):
@@ -269,49 +297,116 @@
             device_id=(back(step2[j]), head), device_id_type=MESH,
         )
 
-    for j in range(len(step1)):
-        s1_copy(j).start()
-    for which in (0, 1):
-        kv_copy(1, which).start()
-    hop1.start()
-    for dz, dc in order:
+    @pl.when(ctx < last)
+    def _():
+        for d in step1:
+            pl.when(ctx + d <= last)(s1_copy(d).start)
+        for which in (0, 1):
+            late_rows(which).start()
+        for which in (0, 1):
+            early_rows(which).start()
+
+    pl.when(ctx + 2 <= last)(hop1.start)
+    for dz, dc in order[:5]:
         q_copy(peer(dz, dc), head).start()
 
-
     same = lambda a, b: jnp.full((2 * n, HD), a, jnp.int32) == jnp.full((2 * n, HD), b, jnp.int32)
-    for j in range(len(step1)):
-        s1_copy(j).wait()
-    mid = sink_own[...].astype(jnp.float32)
-    for j, d in enumerate(step1):
-        mid = mid + jnp.where(same(last_doc[d], last_doc[0]), sink_in1[j].astype(jnp.float32), 0.0)
-    sink_mid[...] = mid.astype(jnp.bfloat16)
-    for j in range(len(step2)):
-        s2_copy(j).start()
-    hop1.wait()
-    hop2.start()
-    for which in (0, 1):
-        kv_copy(1, which).wait()
-    kv_copy(2, 0).start()
+    sink_sum[pl.ds(0, n), :] = sink_k[pl.ds(0, n), :].astype(jnp.float32)
+    sink_sum[pl.ds(n, n), :] = sink_v[pl.ds(0, n), :].astype(jnp.float32)
+    for d in step1:
+
+        @pl.when(ctx >= d)
+        def _(d=d):
+            s1_copy(d).wait_recv()
+            take = same(last_doc[d], doc_a)
+            if d == stride:
+                take = take & (same(doc_before[d], doc_a) == False)
+            sink_sum[...] += jnp.where(take, sink_in1[d - 1].astype(jnp.float32), 0.0)
+
+    def relay_on():
+        hop1.wait_recv()
+        hop2.start()
+
+    pl.when(above + 2 <= last)(relay_on)
+
+    sink_mid[...] = sink_sum[...].astype(jnp.bfloat16)
+    for j, d in enumerate(step2):
+        pl.when(ctx + d <= last)(s2_copy(j).start)
+
+    def send_far_keys():
+        @pl.when(ctx < last)
+        def _():
+            for which in (0, 1):
+                late_rows(which).wait_send()
+                early_rows(which).wait_send()
+
+        pl.when(ctx + 2 <= last)(far_keys.start)
+
+    def send_far_queries():
+        for dz, dc in order[1:5]:
+            q_copy(peer(dz, dc), head).wait_send()
+        for dz, dc in order[5:]:
+            q_copy(peer(dz, dc), head).start()
+
+    def at_block(i, blocks):
+        return pl.multiple_of(i * chunk + blocks * chunk, chunk)
+
+    @pl.when(ctx >= 1)
+    def _():
+        for which in (0, 1):
+            late_rows(which).wait_recv()
+
     own_q.wait()
-    early = 4
-    recent = rows - chunk
+    per_shard = rows // chunk
+    first_reach = per_shard - cut // chunk
+    early, middle = 4, 6
     pipeline(
-        0, early, rows, lambda i: pl.multiple_of(near - recent + i * chunk, chunk), False, "first", True
-    )
-    for j in range(len(step2)):
-        s2_copy(j).wait()
-    got = jnp.zeros((2 * n, HD), jnp.float32)
+        0, early, (first_reach + 1) * chunk, lambda i: at_block(i, 2 * per_shard - first_reach), False, "first", True,
+        (lambda: None, send_far_keys, send_far_queries),
+    )
+
+    @pl.when(ctx >= 1)
+    def _():
+        for which in (0, 1):
+            early_rows(which).wait_recv()
+
     for j, d in enumerate(step2):
-        got = got + jnp.where(same(last_doc[d], doc_a), sink_in2[j].astype(jnp.float32), 0.0)
-    sink_k[pl.ds(0, n), :] = (sink_k[pl.ds(0, n), :].astype(jnp.float32) + got[:n]).astype(jnp.bfloat16)
-    sink_v[pl.ds(0, n), :] = (sink_v[pl.ds(0, n), :].astype(jnp.float32) + got[n:]).astype(jnp.bfloat16)
-
-    kv_copy(2, 0).wait()
-    hop2.wait()
-    pipeline(0, early, near - recent, lambda i: pl.multiple_of(i * chunk, chunk), True, "last", False)
-    pipeline(early, head_n, near + chunk, lambda i: pl.multiple_of(i * chunk, chunk), True, "only", True)
+
+        @pl.when(ctx >= d)
+        def _(j=j, d=d):
+            s2_copy(j).wait_recv()
+            sink_sum[...] += jnp.where(same(doc_before[d], doc_a), sink_in2[j].astype(jnp.float32), 0.0)
+
+    sink_k[pl.ds(0, n), :] = sink_sum[pl.ds(0, n), :].astype(jnp.bfloat16)
+    sink_v[pl.ds(0, n), :] = sink_sum[pl.ds(n, n), :].astype(jnp.bfloat16)
+
+    pipeline(early, middle, rows + chunk, lambda i: at_block(i, per_shard), True, "first", True)
+
+    @pl.when(ctx >= 2)
+    def _():
+        far_keys.wait_recv()
+        hop2.wait_recv()
+
+    pipeline(0, early, near - first_reach * chunk, lambda i: at_block(i, 0), True, "last", False)
+    pipeline(early, middle, rows, lambda i: at_block(i, 0), False, "last", False)
+    pipeline(middle, head_n, near + chunk, lambda i: at_block(i, 0), True, "only", True)
     for i in range(head_n):
         o_copy(i).wait()
+
+    for d in step1:
+        pl.when(ctx + d <= last)(s1_copy(d).wait_send)
+    for j, d in enumerate(step2):
+        pl.when(ctx + d <= last)(s2_copy(j).wait_send)
+
+    for dz, dc in order[:1] + order[5:]:
+        q_copy(peer(dz, dc), head).wait_send()
+
+    @pl.when(ctx + 2 <= last)
+    def _():
+        far_keys.wait_send()
+        hop1.wait_send()
+
+    pl.when(above + 2 <= last)(hop2.wait_send)
 
 
 def per_device(ctx_n, head_n, q_rows, key_rows, value_rows, doc_lengths, window_widths, sink_widths):
@@ -324,9 +419,9 @@
     dma = pltpu.SemaphoreType.DMA
     return pl.pallas_call(
         functools.partial(kernel, ctx_n, head_n, docs),
-        out_shape=jax.ShapeDtypeStruct((rows, QPG * HD), bf),
+        out_shape=pltpu.VMEM((rows, QPG * HD), bf),
         in_specs=[pl.BlockSpec(memory_space=pltpu.HBM)] * 6,
-        out_specs=pl.BlockSpec(memory_space=pltpu.HBM),
+        out_specs=pl.BlockSpec(memory_space=pl.ANY),
         scratch_shapes=[
             pltpu.VMEM((head_n, chunk, QPG * HD), bf),
             pltpu.VMEM((span, HD), bf),
@@ -339,12 +434,13 @@
             pltpu.VMEM((HD, HD), bf),
             pltpu.VMEM((HD, HD), bf),
             pltpu.VMEM((2 * n, HD), bf),
+            pltpu.VMEM((4, 2 * n, HD), bf),
+            pltpu.VMEM((2 * n, HD), jnp.float32),
+            pltpu.VMEM((2 * n, HD), bf),
             pltpu.VMEM((3, 2 * n, HD), bf),
-            pltpu.VMEM((2 * n, HD), bf),
-            pltpu.VMEM((4, 2 * n, HD), bf),
             pltpu.VMEM((rows, HD), bf),
-            pltpu.VMEM((4, chunk * QPG, 2 * HD), jnp.float32),
-            pltpu.VMEM((4, chunk * QPG, HD), jnp.float32),
+            pltpu.VMEM((6, chunk * QPG, 2 * HD), jnp.float32),
+            pltpu.VMEM((6, chunk * QPG, HD), jnp.float32),
             pltpu.SMEM(doc_lengths.shape, jnp.int32),
             pltpu.SMEM(window_widths.shape, jnp.int32),
             pltpu.SMEM(sink_widths.shape, jnp.int32),
@@ -353,18 +449,18 @@
             dma((2,)),
             dma((head_n,)),
             dma((head_n,)),
-            dma((2, 2)),
-            dma((2, 2)),
+            dma((3, 2)),
+            dma((3, 2)),
             dma((2,)),
             dma,
+            dma((4,)),
+            dma((4,)),
             dma((3,)),
             dma((3,)),
-            dma((4,)),
-            dma((4,)),
             dma((head_n,)),
         ],
         compiler_params=pltpu.CompilerParams(
-            collective_id=0, has_side_effects=True, vmem_limit_bytes=48 * 2**20
+            collective_id=0, has_side_effects=True, vmem_limit_bytes=56 * 2**20
         ),
         cost_estimate=pl.CostEstimate(
             flops=4 * rows * QPG * HD * (WSPAN * rows + 2 * chunk),
@@ -372,7 +468,10 @@
             transcendentals=rows * QPG * (WSPAN * rows + 2 * chunk),
         ),
         name="attention",
-    )(doc_lengths, window_widths, sink_widths, q_rows, key_rows, value_rows)
+    )(*[
+        pltpu.with_memory_space_constraint(a, pltpu.HBM)
+        for a in (doc_lengths, window_widths, sink_widths, q_rows, key_rows, value_rows)
+    ])
 
 
 def solution(mesh):

time: 60.3 us -> 51.6 us (0.86)
  the two profiles are of different devices: /device:TPU:0 before, /device:TPU:6 now
where the time goes in v3:
time: 51.6 us; the launch traced here: 51.4 us
  Pallas kernels  50.1 us (97%)
  local copies, waits for them, and re-layouts  1.32 us (3%)
    pallas_call x1, Pallas kernels, per_device(): pl.pallas_call(functools.partial(kernel, ctx_n, head_n, docs), out_shape=...  50.1 us
    unnamed x1, local copies, waits for them, and re-layouts  1.32 us

profile of v3, /device:TPU:6, one launch (start us, length us, event | category | flops | bytes accessed | tf_op | source)
XLA Modules:
  0.0 51.4 jit_solution(9140515456055661017)
XLA Ops:
  0.0 50.1 %attention.1 = bf16[1024,1024]{1,0:T(8,128)(2,1)S(1)} custom-call(s32[16]{0:T(128)} %lengths_hbm.1, s32[8]{0:T(128)} %windows_hbm.1, s32[8]{0:T(128)} %sinks_hbm.1, bf16[128,8192]{1,0:T(8,128)(2,1)} %q_hbm.1, bf16[1024,128]{1,0:T(8,128)(2,1)} %k_hbm.1, bf16[1024,128]{1,0:T(8,128)(2,1)} %v_hbm.1), custom_call_target="tpu_custom_call" | custom-call | flops 9663676416 | bytes 4718592 | tf_op jit(solution)/shard_map/attention/pallas_call | solution.py:420
  50.1 1.3 %copy.8 = bf16[1024,1024]{1,0:T(8,128)(2,1)} copy(bf16[1024,1024]{1,0:T(8,128)(2,1)S(1)} %attention.1) | data formatting | bytes 4194304

commit v4 on v3

--- a/solution.py
+++ b/solution.py
@@ -193,35 +193,45 @@
                     a * chunk : (a + 1) * chunk
                 ]
 
-        def body(s, carry):
-            slot = lax.rem(s - lo, 2)
-            later = jnp.where(s + 1 < hi, s + 1, s)
-            i, j = place(s), place(later)
+        def wait_for(s):
+            if wait_queries:
+                i = place(s)
+                q_copy(i, i).wait_recv()
+
+        def body(step, carry):
+            s = lo + 2 * step
+            more = s + 2 < hi
+            later = jnp.where(more, s + 2, s + 1)
             for k, action in enumerate(on_the_way):
-                pl.when(s == lo + k)(action)
-            if wait_queries:
-
-                @pl.when(s + 1 < hi)
-                def _():
-                    q_copy(j, j).wait_recv()
-
-            set_bias(j, 1 - slot)
+                pl.when(step == k)(action)
+            wait_for(s + 1)
+            if hi - lo > 2:
+                pl.when(more)(functools.partial(wait_for, s + 2))
+            set_bias(place(s + 1), 1)
+            tiles = [(s + d, place(s + d), d, h) for d in (0, 1) for h in range(0, QPG, 2)]
             scores = held[:, pl.ds(0, total)]
-            for h in range(0, QPG, 2):
-                ahead = score(i, slot, h + 2) if h + 2 < QPG else score(j, 1 - slot, 0)
-                finish(s, i, h, scores)
+            for at, (chunk_s, i, slot, h) in enumerate(tiles):
+                if at + 1 < len(tiles):
+                    ahead = score(tiles[at + 1][1], tiles[at + 1][2], tiles[at + 1][3])
+                elif hi - lo > 2:
+                    set_bias(place(later), 0)
+                    ahead = score(place(later), 0, 0)
+                finish(chunk_s, i, h, scores)
                 scores = ahead
-            held[:, pl.ds(0, total)] = scores
-            if stage != "first":
-                o_copy(i).start()
+                if stage != "first" and h + 2 == QPG:
+                    o_copy(i).start()
+            if hi - lo > 2:
+                held[:, pl.ds(0, total)] = scores
             return carry
 
-        i = place(lo)
-        if wait_queries and lo > 0:
-            q_copy(i, i).wait_recv()
-        set_bias(i, 0)
-        held[:, pl.ds(0, total)] = score(i, 0, 0)
-        lax.fori_loop(lo, hi, body, 0)
+        if lo > 0:
+            wait_for(lo)
+        set_bias(place(lo), 0)
+        held[:, pl.ds(0, total)] = score(place(lo), 0, 0)
+        if hi - lo > 2:
+            lax.fori_loop(0, (hi - lo) // 2, body, 0)
+        else:
+            body(0, 0)
 
     def o_copy(i):
         span = pl.ds(pl.multiple_of(i * chunk, chunk), chunk)
@@ -323,12 +333,6 @@
                 take = take & (same(doc_before[d], doc_a) == False)
             sink_sum[...] += jnp.where(take, sink_in1[d - 1].astype(jnp.float32), 0.0)
 
-    def relay_on():
-        hop1.wait_recv()
-        hop2.start()
-
-    pl.when(above + 2 <= last)(relay_on)
-
     sink_mid[...] = sink_sum[...].astype(jnp.bfloat16)
     for j, d in enumerate(step2):
         pl.when(ctx + d <= last)(s2_copy(j).start)
@@ -351,6 +355,12 @@
     def at_block(i, blocks):
         return pl.multiple_of(i * chunk + blocks * chunk, chunk)
 
+    def relay_on():
+        hop1.wait_recv()
+        hop2.start()
+
+    pl.when(above + 2 <= last)(relay_on)
+
     @pl.when(ctx >= 1)
     def _():
         for which in (0, 1):
@@ -359,10 +369,9 @@
     own_q.wait()
     per_shard = rows // chunk
     first_reach = per_shard - cut // chunk
-    early, middle = 4, 6
+    early, middle = 2, 6
     pipeline(
-        0, early, (first_reach + 1) * chunk, lambda i: at_block(i, 2 * per_shard - first_reach), False, "first", True,
-        (lambda: None, send_far_keys, send_far_queries),
+        0, early, (first_reach + 1) * chunk, lambda i: at_block(i, 2 * per_shard - first_reach), False, "first", True
     )
 
     @pl.when(ctx >= 1)
@@ -380,7 +389,11 @@
     sink_k[pl.ds(0, n), :] = sink_sum[pl.ds(0, n), :].astype(jnp.bfloat16)
     sink_v[pl.ds(0, n), :] = sink_sum[pl.ds(n, n), :].astype(jnp.bfloat16)
 
-    pipeline(early, middle, rows + chunk, lambda i: at_block(i, per_shard), True, "first", True)
+    send_far_keys()
+    pipeline(
+        early, middle, rows + chunk, lambda i: at_block(i, per_shard), True, "first", True,
+        (lambda: None, send_far_queries),
+    )
 
     @pl.when(ctx >= 2)
     def _():

time: 51.6 us -> 50.9 us (0.986)
  Pallas kernels: 50.1 us -> 49.4 us
    pallas_call x1, Pallas kernels: 50.1 us -> 49.4 us  [per_device(): pl.pallas_call(functools.partial(kernel, ctx_n, head_n, docs), out_shape=...]
where the time goes in v4:
time: 50.9 us; the launch traced here: 50.7 us
  Pallas kernels  49.4 us (97%)
  local copies, waits for them, and re-layouts  1.32 us (3%)
    pallas_call x1, Pallas kernels, per_device(): pl.pallas_call(functools.partial(kernel, ctx_n, head_n, docs), out_shape=...  49.4 us
    unnamed x1, local copies, waits for them, and re-layouts  1.32 us

profile of v4, /device:TPU:6, one launch (start us, length us, event | category | flops | bytes accessed | tf_op | source)
XLA Modules:
  0.0 50.7 jit_solution(6739885450702441695)
XLA Ops:
  0.0 49.4 %attention.1 = bf16[1024,1024]{1,0:T(8,128)(2,1)S(1)} custom-call(s32[16]{0:T(128)} %lengths_hbm.1, s32[8]{0:T(128)} %windows_hbm.1, s32[8]{0:T(128)} %sinks_hbm.1, bf16[128,8192]{1,0:T(8,128)(2,1)} %q_hbm.1, bf16[1024,128]{1,0:T(8,128)(2,1)} %k_hbm.1, bf16[1024,128]{1,0:T(8,128)(2,1)} %v_hbm.1), custom_call_target="tpu_custom_call" | custom-call | flops 9663676416 | bytes 4718592 | tf_op jit(solution)/shard_map/attention/pallas_call | solution.py:433
  49.4 1.3 %copy.8 = bf16[1024,1024]{1,0:T(8,128)(2,1)} copy(bf16[1024,1024]{1,0:T(8,128)(2,1)S(1)} %attention.1) | data formatting | bytes 4194304

commit v5 on v4

--- a/solution.py
+++ b/solution.py
@@ -218,10 +218,11 @@
                     ahead = score(place(later), 0, 0)
                 finish(chunk_s, i, h, scores)
                 scores = ahead
-                if stage != "first" and h + 2 == QPG:
-                    o_copy(i).start()
             if hi - lo > 2:
                 held[:, pl.ds(0, total)] = scores
+            if stage != "first":
+                o_copy(place(s)).start()
+                o_copy(place(s + 1)).start()
             return carry
 
         if lo > 0:

time: 50.9 us -> 48.8 us (0.959)
  Pallas kernels: 49.4 us -> 47.4 us
    pallas_call x1, Pallas kernels: 49.4 us -> 47.4 us  [per_device(): pl.pallas_call(functools.partial(kernel, ctx_n, head_n, docs), out_shape=...]
where the time goes in v5:
time: 48.8 us; the launch traced here: 48.7 us
  Pallas kernels  47.4 us (97%)
  local copies, waits for them, and re-layouts  1.32 us (3%)
    pallas_call x1, Pallas kernels, per_device(): pl.pallas_call(functools.partial(kernel, ctx_n, head_n, docs), out_shape=...  47.4 us
    unnamed x1, local copies, waits for them, and re-layouts  1.32 us

profile of v5, /device:TPU:6, one launch (start us, length us, event | category | flops | bytes accessed | tf_op | source)
XLA Modules:
  0.0 48.7 jit_solution(12814758743109163300)
XLA Ops:
  0.0 47.4 %attention.1 = bf16[1024,1024]{1,0:T(8,128)(2,1)S(1)} custom-call(s32[16]{0:T(128)} %lengths_hbm.1, s32[8]{0:T(128)} %windows_hbm.1, s32[8]{0:T(128)} %sinks_hbm.1, bf16[128,8192]{1,0:T(8,128)(2,1)} %q_hbm.1, bf16[1024,128]{1,0:T(8,128)(2,1)} %k_hbm.1, bf16[1024,128]{1,0:T(8,128)(2,1)} %v_hbm.1), custom_call_target="tpu_custom_call" | custom-call | flops 9663676416 | bytes 4718592 | tf_op jit(solution)/shard_map/attention/pallas_call | solution.py:434
  47.4 1.3 %copy.8 = bf16[1024,1024]{1,0:T(8,128)(2,1)} copy(bf16[1024,1024]{1,0:T(8,128)(2,1)S(1)} %attention.1) | data formatting | bytes 4194304

commit v6 on v5

--- a/solution.py
+++ b/solution.py
@@ -266,7 +266,7 @@
             device_id_type=MESH,
         )
 
-    cut = 3 * chunk
+    cut = 5 * chunk
 
     def kv_copy(d, which, lo, count, sem):
         src = (k_hbm, v_hbm)[which]

time: 48.8 us -> 49.5 us (1.014)
  Pallas kernels: 47.4 us -> 48 us
    pallas_call x1, Pallas kernels: 47.4 us -> 48 us  [per_device(): pl.pallas_call(functools.partial(kernel, ctx_n, head_n, docs), out_shape=...]
where the time goes in v6:
time: 49.5 us; the launch traced here: 49.4 us
  Pallas kernels  48 us (97%)
  local copies, waits for them, and re-layouts  1.32 us (3%)
    pallas_call x1, Pallas kernels, per_device(): pl.pallas_call(functools.partial(kernel, ctx_n, head_n, docs), out_shape=...  48 us
    unnamed x1, local copies, waits for them, and re-layouts  1.32 us

profile of v6, /device:TPU:6, one launch (start us, length us, event | category | flops | bytes accessed | tf_op | source)
XLA Modules:
  0.0 49.4 jit_solution(8003609573842334588)
XLA Ops:
  0.0 48.0 %attention.1 = bf16[1024,1024]{1,0:T(8,128)(2,1)S(1)} custom-call(s32[16]{0:T(128)} %lengths_hbm.1, s32[8]{0:T(128)} %windows_hbm.1, s32[8]{0:T(128)} %sinks_hbm.1, bf16[128,8192]{1,0:T(8,128)(2,1)} %q_hbm.1, bf16[1024,128]{1,0:T(8,128)(2,1)} %k_hbm.1, bf16[1024,128]{1,0:T(8,128)(2,1)} %v_hbm.1), custom_call_target="tpu_custom_call" | custom-call | flops 9663676416 | bytes 4718592 | tf_op jit(solution)/shard_map/attention/pallas_call | solution.py:434
  48.0 1.3 %copy.8 = bf16[1024,1024]{1,0:T(8,128)(2,1)} copy(bf16[1024,1024]{1,0:T(8,128)(2,1)S(1)} %attention.1) | data formatting | bytes 4194304
